TPU v7x, 256 devices: a whole 4x4x8 slice. The times are simulated.
256 devices in a mesh: row: 8 (over y, core), col: 32 (over x, z).
Axes of the slice: x: 4, y: 4, z: 8, core: 2. Of those that a mesh axis runs over, the one named last changes fastest.
Arguments:
- history: bfloat16 [2, 2, 512, 32, 16384], P(None, None, 'row', None, 'col'), may hold values from -6 to 6
- sigma_rows: bfloat16 [2, 2, 32, 16384], P(None, None, None, 'row'), may hold values from -0.03125 to 0.03125
- propagator: bfloat16 [2, 32, 32], replicated, may hold values from -0.75 to 0.75
- block_map: int32 [64], replicated, may hold values from 0 to 63, each once
- step_index: int32 [1], replicated, may hold values from 1 to 510
Outputs:
- new_rows: float32 [2, 2, 2, 32, 16384], P(None, None, None, None, 'col')
- mirror: bfloat16 [2, 2, 2, 512, 1024], P(None, None, None, 'row')
Inputs may be any that keep to these rules, and one draw needn't show every extreme that they name: block_map is a permutation of the 64 time blocks.
All inputs are finite; a program needn't handle non-finite values.
Results may differ from a plain program's by a relative error of at most 0.009.
Values may be sent and summed in bfloat16 or wider, within the bound.
No kernel may reach another device: no remote copies, remote signals or barrier semaphores. Data moves between devices by JAX's collectives and lax.ppermute only.
A program may use at most 64 MiB of HBM per device.

v0:
```python
import jax
import jax.numpy as jnp
from jax import lax
from jax.sharding import PartitionSpec as P

TB = 8


def broadcast(value, axis, source):
    kept = jnp.where(lax.axis_index(axis) == source, value, 0).astype(value.dtype)
    return lax.psum(kept, axis)


def stacked_rows(real_part, imag_part):
    upper_half = jnp.concatenate([real_part, -imag_part], axis=-1)
    lower_half = jnp.concatenate([imag_part, real_part], axis=-1)
    return jnp.concatenate([upper_half, lower_half], axis=-2)


def turn_back(values):
    return jnp.stack([values[:, 1], -values[:, 0]], axis=1)


def apply_matrix(matrix, row_data):
    kinds = row_data.shape[0]
    flat = row_data.reshape(kinds, matrix.shape[1], row_data.shape[-1])
    result = jnp.einsum("ab,xbt->xat", matrix, flat, preferred_element_type=jnp.float32)
    return result.reshape(row_data.shape)


def step_weights(time_rows, current):
    beyond = time_rows > current
    edge_one = (time_rows == 0) | (time_rows == current)
    weight_one = jnp.where(beyond, 0.0, jnp.where(edge_one, 0.5, 1.0))
    weight_two = jnp.where(beyond, 0.0, jnp.where(time_rows == 0, 0.5, 1.0))
    return jnp.stack([weight_one, weight_two]).astype(jnp.bfloat16)


def per_device(history, sigma_rows, propagator, block_map, step_index):
    orbitals = history.shape[3]
    own_rows = history.shape[2]
    columns = history.shape[4]
    first_row = lax.axis_index("row") * own_rows
    local_blocks = own_rows // TB
    held_blocks = lax.dynamic_slice_in_dim(block_map, first_row // TB, local_blocks)
    offsets = jnp.arange(TB, dtype=jnp.int32)
    held_times = (held_blocks[:, None] * TB + offsets[None, :]).reshape(-1)
    current = step_index[0]
    weights = jnp.repeat(step_weights(held_times, current), orbitals, axis=1)
    weighted = sigma_rows * weights[:, None, None, :]
    stacked = stacked_rows(weighted[:, 0], weighted[:, 1]).reshape(
        4 * orbitals, 2 * own_rows * orbitals
    )
    kinds_flat = history.reshape(2, 2 * own_rows * orbitals, columns)
    products = jnp.einsum("ak,xkt->xat", stacked, kinds_flat, preferred_element_type=jnp.float32)
    products = products.reshape(2, 2, 2, orbitals, columns)
    block_slots = jnp.arange(block_map.shape[0], dtype=jnp.int32)

    def position(time_value):
        home_block = jnp.sum(jnp.where(block_map == time_value // TB, block_slots, 0))
        return home_block * TB + time_value % TB

    propagate = stacked_rows(propagator[0], propagator[1])
    local_now = position(current) - first_row
    holds_now = (local_now >= 0) & (local_now < own_rows)
    now_row = lax.dynamic_index_in_dim(
        history, jnp.clip(local_now, 0, own_rows - 1), 2, keepdims=False
    )
    advanced = apply_matrix(propagate, now_row)
    part_first = turn_back(products[:, 0]) + jnp.where(holds_now, advanced, 0.0)
    local_next = position(current + 1) - first_row
    holds_next = (local_next >= 0) & (local_next < own_rows)
    diagonal = lax.dynamic_slice_in_dim(
        sigma_rows[1], jnp.clip(local_next, 0, own_rows - 1) * orbitals, orbitals, 2
    )
    half_diagonal = diagonal * 0.5
    new_first = lax.psum(part_first, "row")
    first_low = new_first.astype(jnp.bfloat16)
    diag_term = apply_matrix(stacked_rows(half_diagonal[0], half_diagonal[1]), first_low)
    part_second = turn_back(products[:, 1] + jnp.where(holds_next, diag_term, 0.0))
    new_second = lax.psum(part_second.astype(jnp.bfloat16), "row").astype(
        jnp.float32
    ) + apply_matrix(propagate, first_low)
    new_rows = jnp.stack([new_first, new_second])
    col_times = columns // orbitals
    flipped = new_rows.astype(jnp.bfloat16).reshape(8, orbitals, col_times, orbitals)
    flipped = flipped.transpose(0, 2, 3, 1).reshape(8, col_times, orbitals * orbitals)
    flip_signs = jnp.tile(jnp.array([-1.0, 1.0], jnp.bfloat16), 4)
    mirrored = flipped * flip_signs[:, None, None]

    def fetch_block(block_index, gathered):
        block_id = held_blocks[block_index]
        root_col = block_id * TB // col_times
        start_row = block_id * TB % col_times
        piece = lax.dynamic_slice_in_dim(mirrored, start_row, TB, 1)
        received = broadcast(piece, "col", root_col)
        return lax.dynamic_update_slice_in_dim(gathered, received, block_index * TB, 1)

    empty = jnp.zeros((8, own_rows, orbitals * orbitals), jnp.bfloat16)
    mirror = lax.fori_loop(0, local_blocks, fetch_block, empty)
    return (new_rows, mirror.reshape(2, 2, 2, own_rows, orbitals * orbitals))


def solution(mesh):
    return jax.shard_map(
        per_device,
        mesh=mesh,
        in_specs=(P(None, None, "row", None, "col"), P(None, None, None, "row"), P(), P(), P()),
        out_specs=(P(None, None, None, None, "col"), P(None, None, None, "row", None)),
        check_vma=False,
    )
```

profile of v0, /device:TPU:1, one launch (start us, length us, event | category | flops | bytes accessed | tf_op | source)
XLA Modules:
  0.0 1323.5 jit_solution(16074063132557455951)
XLA Ops:
  7.9 1.4 fusion.14
  10.0 0.7 fusion.18
  10.7 0.7 slice_bitcast_fusion.6
  11.4 0.7 broadcast_multiply_fusion.2
  12.6 1.1 broadcast_multiply_fusion
  13.8 0.9 constant_dynamic-slice_fusion
  14.8 4.6 fusion.23
  19.7 0.7 maximum_add_fusion
  21.5 66.0 %all-reduce.4.cloned.1.call-done = f32[2,2,32,512]{3,2,1,0:T(8,128)} async-done(((f32[2,2,32,512]{3,2,1,0:T(8,128)}), f32[2,2,32,512]{3,2,1,0:T(8,128)}) %all-reduce.4.cloned.1.call-update) | async-done | bytes 262160 | tf_op jit(solution)/shard_map/psum | solution.py:77
  87.4 1.0 convert_element_type.23
  88.8 0.7 pad_maximum_fusion.1
  89.7 64.2 %all-reduce.6.cloned.1.call-done = bf16[2,2,32,512]{3,2,1,0:T(8,128)(2,1)} async-done(((bf16[2,2,32,512]{3,2,1,0:T(8,128)(2,1)}), bf16[2,2,32,512]{3,2,1,0:T(8,128)(2,1)}) %all-reduce.6.cloned.1.call-update) | async-done | bytes 131088 | tf_op jit(solution)/shard_map/psum | solution.py:81
  153.9 0.9 add_bitcast_fusion
  154.9 0.9 fusion.21
  156.3 1.0 copy.15
  157.3 1.1 reshape.127
  158.7 1157.0 %while.15 = (s32[]{:T(128)}, bf16[8,64,1024]{2,1,0:T(8,128)(2,1)S(1)}, s32[8]{0:T(128)S(1)}, bf16[8,16,1024]{2,1,0:T(8,128)(2,1)S(1)}, s32[]{:T(128)}, /*index=5...) while((s32[]{:T(128)}, ...), condition=%wide.region_6.7_spmd, body=%wide.region_4.6_spmd.sunk | while | flops 131104 | bytes 1311230 | solution.py:100
  158.7 0.6 dynamic_slice.40
  160.0 0.7 dynamic-slice_select_fusion.2
  160.7 141.0 %all-reduce.8.cloned.1.call-done = bf16[8,8,1024]{2,1,0:T(8,128)(2,1)} async-done(((bf16[8,8,1024]{2,1,0:T(8,128)(2,1)}), bf16[8,8,1024]{2,1,0:T(8,128)(2,1)}) %all-reduce.8.cloned.1.call-update) | async-done | bytes 131088 | tf_op jit(solution)/shard_map/while/body/eval_jaxpr/psum | solution.py:11
  301.7 0.9 constant_dynamic-update-slice_fusion.2
  302.7 0.6 dynamic_slice.40
  304.0 0.7 dynamic-slice_select_fusion.2
  304.7 141.6 %all-reduce.8.cloned.1.call-done = bf16[8,8,1024]{2,1,0:T(8,128)(2,1)} async-done(((bf16[8,8,1024]{2,1,0:T(8,128)(2,1)}), bf16[8,8,1024]{2,1,0:T(8,128)(2,1)}) %all-reduce.8.cloned.1.call-update) | async-done | bytes 131088 | tf_op jit(solution)/shard_map/while/body/eval_jaxpr/psum | solution.py:11
  446.3 0.9 constant_dynamic-update-slice_fusion.2
  447.3 0.6 dynamic_slice.40
  448.6 0.7 dynamic-slice_select_fusion.2
  449.3 141.6 %all-reduce.8.cloned.1.call-done = bf16[8,8,1024]{2,1,0:T(8,128)(2,1)} async-done(((bf16[8,8,1024]{2,1,0:T(8,128)(2,1)}), bf16[8,8,1024]{2,1,0:T(8,128)(2,1)}) %all-reduce.8.cloned.1.call-update) | async-done | bytes 131088 | tf_op jit(solution)/shard_map/while/body/eval_jaxpr/psum | solution.py:11
  590.9 0.9 constant_dynamic-update-slice_fusion.2
  591.9 0.6 dynamic_slice.40
  593.2 0.7 dynamic-slice_select_fusion.2
  593.9 141.6 %all-reduce.8.cloned.1.call-done = bf16[8,8,1024]{2,1,0:T(8,128)(2,1)} async-done(((bf16[8,8,1024]{2,1,0:T(8,128)(2,1)}), bf16[8,8,1024]{2,1,0:T(8,128)(2,1)}) %all-reduce.8.cloned.1.call-update) | async-done | bytes 131088 | tf_op jit(solution)/shard_map/while/body/eval_jaxpr/psum | solution.py:11
  735.5 0.9 constant_dynamic-update-slice_fusion.2
  736.5 0.6 dynamic_slice.40
  737.8 0.7 dynamic-slice_select_fusion.2
  738.5 141.9 %all-reduce.8.cloned.1.call-done = bf16[8,8,1024]{2,1,0:T(8,128)(2,1)} async-done(((bf16[8,8,1024]{2,1,0:T(8,128)(2,1)}), bf16[8,8,1024]{2,1,0:T(8,128)(2,1)}) %all-reduce.8.cloned.1.call-update) | async-done | bytes 131088 | tf_op jit(solution)/shard_map/while/body/eval_jaxpr/psum | solution.py:11
  880.4 0.9 constant_dynamic-update-slice_fusion.2
  881.4 0.6 dynamic_slice.40
  882.7 0.7 dynamic-slice_select_fusion.2
  883.4 141.9 %all-reduce.8.cloned.1.call-done = bf16[8,8,1024]{2,1,0:T(8,128)(2,1)} async-done(((bf16[8,8,1024]{2,1,0:T(8,128)(2,1)}), bf16[8,8,1024]{2,1,0:T(8,128)(2,1)}) %all-reduce.8.cloned.1.call-update) | async-done | bytes 131088 | tf_op jit(solution)/shard_map/while/body/eval_jaxpr/psum | solution.py:11
  1025.3 0.9 constant_dynamic-update-slice_fusion.2
  1027.6 0.7 dynamic-slice_select_fusion.2
  1028.3 141.9 %all-reduce.8.cloned.1.call-done = bf16[8,8,1024]{2,1,0:T(8,128)(2,1)} async-done(((bf16[8,8,1024]{2,1,0:T(8,128)(2,1)}), bf16[8,8,1024]{2,1,0:T(8,128)(2,1)}) %all-reduce.8.cloned.1.call-update) | async-done | bytes 131088 | tf_op jit(solution)/shard_map/while/body/eval_jaxpr/psum | solution.py:11
  1170.2 0.9 constant_dynamic-update-slice_fusion.2
  1172.4 0.7 dynamic-slice_select_fusion.2
  1173.2 141.6 %all-reduce.8.cloned.1.call-done = bf16[8,8,1024]{2,1,0:T(8,128)(2,1)} async-done(((bf16[8,8,1024]{2,1,0:T(8,128)(2,1)}), bf16[8,8,1024]{2,1,0:T(8,128)(2,1)}) %all-reduce.8.cloned.1.call-update) | async-done | bytes 131088 | tf_op jit(solution)/shard_map/while/body/eval_jaxpr/psum | solution.py:11
  1314.8 0.9 constant_dynamic-update-slice_fusion.2
  1315.7 1.0 copy-done.1
  (54 shorter events, 4.1 us)
Async XLA Ops:
  7.2 80.3 %all-reduce.4.cloned.1.call-start = ((), (), s32[]{:S(2)}) async-start(), calls=%async_computation | async-start | bytes 524288 | tf_op jit(solution)/shard_map/psum | solution.py:77
  19.4 1.8 copy-start.2
  19.4 1.9 slice-start
  20.5 133.4 %all-reduce.6.cloned.1.call-start = ((), (), s32[]{:S(2)}) async-start(), calls=%async_computation.1 | async-start | bytes 262144 | tf_op jit(solution)/shard_map/psum | solution.py:81
  87.4 67.4 %copy-start = (f32[2,2,32,512]{3,2,1,0:T(8,128)S(1)}, f32[2,2,32,512]{3,2,1,0:T(8,128)}, u32[]{:S(2)}) copy-start(f32[2,2,32,512]{3,2,1,0:T(8,128)} %all-reduce.4.cloned.1.call-done) | copy-start | bytes 786436
  158.7 143.1 %all-reduce.8.cloned.1.call-start = ((), (), s32[]{:S(2)}) async-start(), calls=%async_computation.2 | async-start | bytes 262144 | tf_op jit(solution)/shard_map/while/body/eval_jaxpr/psum | solution.py:11
  302.7 143.7 %all-reduce.8.cloned.1.call-start = ((), (), s32[]{:S(2)}) async-start(), calls=%async_computation.2 | async-start | bytes 262144 | tf_op jit(solution)/shard_map/while/body/eval_jaxpr/psum | solution.py:11
  447.2 143.7 %all-reduce.8.cloned.1.call-start = ((), (), s32[]{:S(2)}) async-start(), calls=%async_computation.2 | async-start | bytes 262144 | tf_op jit(solution)/shard_map/while/body/eval_jaxpr/psum | solution.py:11
  591.8 143.7 %all-reduce.8.cloned.1.call-start = ((), (), s32[]{:S(2)}) async-start(), calls=%async_computation.2 | async-start | bytes 262144 | tf_op jit(solution)/shard_map/while/body/eval_jaxpr/psum | solution.py:11
  736.4 144.0 %all-reduce.8.cloned.1.call-start = ((), (), s32[]{:S(2)}) async-start(), calls=%async_computation.2 | async-start | bytes 262144 | tf_op jit(solution)/shard_map/while/body/eval_jaxpr/psum | solution.py:11
  881.3 144.0 %all-reduce.8.cloned.1.call-start = ((), (), s32[]{:S(2)}) async-start(), calls=%async_computation.2 | async-start | bytes 262144 | tf_op jit(solution)/shard_map/while/body/eval_jaxpr/psum | solution.py:11
  1026.2 143.9 %all-reduce.8.cloned.1.call-start = ((), (), s32[]{:S(2)}) async-start(), calls=%async_computation.2 | async-start | bytes 262144 | tf_op jit(solution)/shard_map/while/body/eval_jaxpr/psum | solution.py:11
  1171.1 143.7 %all-reduce.8.cloned.1.call-start = ((), (), s32[]{:S(2)}) async-start(), calls=%async_computation.2 | async-start | bytes 262144 | tf_op jit(solution)/shard_map/while/body/eval_jaxpr/psum | solution.py:11
  1315.7 1.0 copy-start.1
Sparse Core Ops, SparseCore 0:
  20.6 66.7 all-reduce.3
  90.4 63.4 all-reduce.5
  163.5 138.1 all-reduce.7
  307.2 139.0 all-reduce.7
  451.8 139.0 all-reduce.7
  596.4 139.0 all-reduce.7
  741.3 139.0 all-reduce.7
  886.2 139.0 all-reduce.7
  1031.1 139.0 all-reduce.7
  1175.7 139.0 all-reduce.7
where the time goes:
time: 1330 us; the launch traced here: 1320 us
  waiting for transfers between devices  1260 us (95%)
  local copies, waits for them, and re-layouts  17.9 us (1%)
  between operations  16.4 us (1%)
  other arithmetic  14.3 us (1%)
    psum x8, waiting for transfers between devices, broadcast(): return lax.psum(kept, axis)  1130 us
    psum x1, waiting for transfers between devices, per_device(): new_first = lax.psum(part_first, 'row')  66 us
    psum x1, waiting for transfers between devices, per_device(): lax.psum(part_second.astype(jnp.bfloat16), 'row').astype(jnp.float32)  64.2 us
  transfers between devices with their start and end apart: 10, of which 10 were waited for; matrix products, arithmetic and copies ran while one was open for 0% of the time, Pallas kernels for 0%

commit v1 on v0

v1 whole, which is shorter than its diff:
```python
import jax
import jax.numpy as jnp
from jax import lax
from jax.experimental import pallas as pl
from jax.experimental.pallas import tpu as pltpu
from jax.sharding import Mesh, PartitionSpec as P

TB = 8
ORB = 32
ROWS = 8
XS = 4
ZS = 8
BF = jnp.bfloat16
F32 = jnp.float32
SLICES = ROWS * XS
DATA = 32
DIAG = 16
BACK = 160


def dot(a, b):
    return jnp.dot(a, b, preferred_element_type=F32)


def dot_nt(a, b):
    return lax.dot_general(a, b, (((1,), (1,)), ((), ())), preferred_element_type=F32)


def iota(shape, axis):
    return lax.broadcasted_iota(jnp.int32, shape, axis)


def one_hot(cond):
    return jnp.where(cond, 1.0, 0.0).astype(BF)


def product_kernel(map_ref, step_ref, hist_ref, sigma_ref, prop_ref, out_ref, acc_ref, diag_ref):
    k = pl.program_id(0)
    row = lax.axis_index("row")
    current = step_ref[0]
    block = map_ref[row * ROWS + k]

    @pl.when(k == 0)
    def _():
        diag_ref[...] = jnp.zeros_like(diag_ref)

    times = block * TB + iota((1, TB * ORB), 1) // ORB
    beyond = times > current
    weight_two = jnp.where(beyond, 0.0, jnp.where(times == 0, 0.5, 1.0))
    weight_one = jnp.where(beyond, 0.0, jnp.where((times == 0) | (times == current), 0.5, 1.0))
    on_real, on_imag = [], []
    for s, weight in enumerate((weight_one, weight_two)):
        real = sigma_ref[s, 0].astype(F32) * weight
        imag = sigma_ref[s, 1].astype(F32) * weight
        on_real += [imag, -real]
        on_imag += [real, imag]
    left = jnp.concatenate(
        [jnp.concatenate(on_real, axis=0), jnp.concatenate(on_imag, axis=0)], axis=1
    ).astype(BF)
    for kind in range(2):
        part = dot(left, hist_ref[kind].reshape(2 * TB * ORB, hist_ref.shape[-1]))

        @pl.when(k == 0)
        def _():
            acc_ref[kind] = part

        @pl.when(k > 0)
        def _():
            acc_ref[kind] += part

    @pl.when(block == current // TB)
    def _():
        at = current % TB
        real, imag = prop_ref[0], prop_ref[1]
        by_real = jnp.concatenate([real, imag], axis=0)
        by_imag = jnp.concatenate([-imag, real], axis=0)
        for kind in range(2):
            acc_ref[kind, : 2 * ORB] += dot(by_real, hist_ref[kind, 0, at]) + dot(
                by_imag, hist_ref[kind, 1, at]
            )

    @pl.when(block == (current + 1) // TB)
    def _():
        first = (current + 1) % TB * ORB
        pick = one_hot(iota((TB * ORB, 128), 0) == first + iota((TB * ORB, 128), 1) % ORB)
        tiled = dot(sigma_ref[1].reshape(2 * ORB, TB * ORB), pick)
        own = iota((2 * ORB, 128), 1) // ORB == iota((2 * ORB, 128), 0) % 4
        fold = one_hot(iota((DIAG, 2 * ORB), 1) // 4 == iota((DIAG, 2 * ORB), 0))
        diag_ref[...] = dot(fold, jnp.where(own, tiled, 0.0).astype(BF)) * 0.5

    @pl.when(k == pl.num_programs(0) - 1)
    def _():
        for kind in range(2):
            turned = acc_ref[kind].T.astype(BF)
            for blk in range(2):
                for part in range(16):
                    first = (blk * 16 + part) * 16
                    out_ref[kind * 16 + part, blk * 16 : blk * 16 + 16, :] = turned[first : first + 16]
        diag = diag_ref[...].astype(BF)
        for part in range(SLICES):
            out_ref[part, DATA:, :] = diag


def finish_kernel(in_ref, prop_ref, rows_ref, mirror_ref):
    sums = []
    for x in range(XS):
        total = in_ref[x, :DATA].astype(F32)
        for r in range(1, ROWS):
            total += in_ref[r * XS + x, :DATA].astype(F32)
        sums.append(total)
    total = jnp.concatenate(sums, axis=0)
    packed = in_ref[0, DATA:].astype(F32)
    for r in range(1, ROWS):
        packed += in_ref[r * XS, DATA:].astype(F32)
    lane = iota((ORB, 128), 1)
    left, right = lane < ORB, (lane >= ORB) & (lane < 2 * ORB)
    nothing = jnp.zeros((2 * ORB, 128), F32)

    def matrix(upper_left, upper_right, lower_left, lower_right):
        upper = jnp.where(left, upper_left, jnp.where(right, upper_right, 0.0))
        lower = jnp.where(left, lower_left, jnp.where(right, lower_right, 0.0))
        return jnp.concatenate([nothing, upper, lower], axis=0).astype(BF)

    tile = one_hot(iota((ORB, 128), 0) == iota((ORB, 128), 1) % ORB)
    real, imag = dot(prop_ref[0], tile), dot(prop_ref[1], tile)
    propagate = matrix(real, -imag, imag, real)
    spread = one_hot(iota((2 * ORB, DIAG), 0) // 4 == iota((2 * ORB, DIAG), 1))
    own = iota((2 * ORB, 128), 1) // ORB == iota((2 * ORB, 128), 0) % 4
    wide = jnp.where(own, dot(spread, packed.astype(BF)), 0.0).astype(BF)
    wrap = one_hot(iota((128, 128), 0) % ORB == iota((128, 128), 1) % ORB)
    diag = dot(wide, wrap)
    d_real, d_imag = diag[:ORB], diag[ORB:]
    turn = matrix(d_imag, d_real, -d_real, d_imag)
    low = total.astype(BF)
    new = (total + dot_nt(low, propagate) + dot_nt(low, turn)).astype(BF)
    rows_ref[...] = new
    size = XS * DATA
    lane_block = iota((size, 128), 1) // ORB
    place = iota((size, 128), 0) % 4
    signed = jnp.where(lane_block % 2 == 0, -new.astype(F32), new.astype(F32))
    result = jnp.where(lane_block == place, signed, 0.0)
    for d in range(1, 4):
        moved = jnp.where(lane_block == place, pltpu.roll(signed, 128 - ORB * d, 1), 0.0)
        result += jnp.where(
            place >= d, pltpu.roll(moved, d, 0), pltpu.roll(moved, size + d - 4, 0)
        )
    result = result.astype(BF)
    for z in range(ZS):
        mirror_ref[z] = result


def select_kernel(map_ref, blocks_ref, rows_ref, out_ref):
    for r in range(ROWS):
        for j in range(TB):
            block = map_ref[r * TB + j]
            column = block // 2
            start = pl.multiple_of(column // ZS * DATA + block % 2 * 16, 16)
            piece = blocks_ref[column % ZS, pl.ds(start, 16), :]
            for x in range(XS):
                out_ref[r * XS + x, j * 16 : j * 16 + 16, :] = piece
        for x in range(XS):
            out_ref[r * XS + x, 128:, :] = rows_ref[x * DATA : x * DATA + DATA, :]


def place_kernel(in_ref, rows_ref, mirror_ref, mixed_ref, tall_ref):
    for h in range(2):
        for pair in range(4):
            for half in range(2):
                j = pair * 2 + half
                for tm in range(TB):
                    mixed_ref[h, pair, pl.ds(half * 8 + tm, 16, stride=16), :] = in_ref[
                        tm * 2 + h, j * 16 : j * 16 + 16, :
                    ].astype(F32)
            for q in range(4):
                for g in range(4):
                    first = (q * 4 + g) * 16
                    mirror_ref[
                        g // 2, 0, g % 2, pair * 16 : pair * 16 + 16, (h * 4 + q) * 128 : (h * 4 + q) * 128 + 128
                    ] = mixed_ref[h, pair, first : first + 16, :].astype(BF)
    for blk in range(2):
        for part in range(16):
            first = (blk * 16 + part) * 16
            tall_ref[first : first + 16, :] = in_ref[part, 128 + blk * 16 : 144 + blk * 16, :].astype(F32)
    wide = tall_ref[...].T
    for g in range(4):
        rows_ref[g // 2, 0, g % 2] = wide[g * ORB : g * ORB + ORB, :]


def per_device(history, sigma_rows, propagator, block_map, step_index):
    smem = pl.BlockSpec(memory_space=pltpu.SMEM)
    vmem = pl.BlockSpec(memory_space=pltpu.VMEM)
    columns = history.shape[4]
    partial = pl.pallas_call(
        product_kernel,
        grid=(ROWS,),
        in_specs=[
            smem,
            smem,
            pl.BlockSpec((2, 2, TB, ORB, columns), lambda k: (0, 0, k, 0, 0)),
            pl.BlockSpec((2, 2, ORB, TB * ORB), lambda k: (0, 0, 0, k)),
            pl.BlockSpec((2, ORB, ORB), lambda k: (0, 0, 0)),
        ],
        out_specs=pl.BlockSpec((SLICES, DATA + DIAG, 128), lambda k: (0, 0, 0)),
        out_shape=jax.ShapeDtypeStruct((SLICES, DATA + DIAG, 128), BF),
        scratch_shapes=[pltpu.VMEM((2, 128, columns), F32), pltpu.VMEM((DIAG, 128), F32)],
        compiler_params=pltpu.CompilerParams(vmem_limit_bytes=24 << 20),
        name="products",
    )(block_map, step_index, history, sigma_rows, propagator)
    partial = lax.all_to_all(partial, ("row", "x"), 0, 0, tiled=True)
    new, copies = pl.pallas_call(
        finish_kernel,
        in_specs=[vmem, vmem],
        out_specs=[vmem, vmem],
        out_shape=[
            jax.ShapeDtypeStruct((XS * DATA, 128), BF),
            jax.ShapeDtypeStruct((ZS, XS * DATA, 128), BF),
        ],
        compiler_params=pltpu.CompilerParams(vmem_limit_bytes=24 << 20),
        name="finish",
    )(partial, propagator)
    blocks = lax.all_to_all(copies, "z", 0, 0, tiled=True)
    back = pl.pallas_call(
        select_kernel,
        in_specs=[smem, vmem, vmem],
        out_specs=vmem,
        out_shape=jax.ShapeDtypeStruct((SLICES, BACK, 128), BF),
        compiler_params=pltpu.CompilerParams(vmem_limit_bytes=24 << 20),
        name="select",
    )(block_map, blocks, new)
    back = lax.all_to_all(back, ("row", "x"), 0, 0, tiled=True)
    new_rows, mirror = pl.pallas_call(
        place_kernel,
        grid=(2,),
        in_specs=[pl.BlockSpec((SLICES // 2, BACK, 128), lambda kind: (kind, 0, 0))],
        out_specs=[
            pl.BlockSpec((2, 1, 2, ORB, columns), lambda kind: (0, kind, 0, 0, 0)),
            pl.BlockSpec((2, 1, 2, ROWS * TB, ORB * ORB), lambda kind: (0, kind, 0, 0, 0)),
        ],
        out_shape=[
            jax.ShapeDtypeStruct((2, 2, 2, ORB, columns), F32),
            jax.ShapeDtypeStruct((2, 2, 2, ROWS * TB, ORB * ORB), BF),
        ],
        scratch_shapes=[pltpu.VMEM((2, 4, 256, 128), F32), pltpu.VMEM((columns, 128), F32)],
        compiler_params=pltpu.CompilerParams(vmem_limit_bytes=24 << 20),
        name="place",
    )(back)
    return new_rows, mirror


def solution(mesh):
    split = Mesh(mesh.devices.reshape(ROWS, XS, ZS), ("row", "x", "z"))
    column = ("x", "z")
    return jax.shard_map(
        per_device,
        mesh=split,
        in_specs=(P(None, None, "row", None, column), P(None, None, None, "row"), P(), P(), P()),
        out_specs=(P(None, None, None, None, column), P(None, None, None, "row", None)),
        check_vma=False,
    )
```

time: 1330 us -> 79.4 us (0.06)
  waiting for transfers between devices: 1260 us -> 0 us
  blocking collectives: 0 us -> 62.6 us
  between operations: 16.4 us -> 1.31 us
  other arithmetic: 14.3 us -> 0 us
    psum x10 -> x0, waiting for transfers between devices: 1260 us -> none  [the longest x8 1130 us: broadcast(): return lax.psum(kept, axis)]
    all_to_all x0 -> x3, blocking collectives: none -> 62.6 us  [the longest x1 25.1 us: per_device(): back = lax.all_to_all(back, ('row', 'x'), 0, 0, tiled=True)]
  transfers between devices with their start and end apart: 10 -> 0, of which waited for: 10 -> 0; matrix products, arithmetic and copies ran while one was open for 0% -> 0% of each run, Pallas kernels for 0% -> 0%
where the time goes in v1:
time: 79.4 us; the launch traced here: 79.1 us
  blocking collectives  62.6 us (79%)
  Pallas kernels  9.4 us (12%)
  local copies, waits for them, and re-layouts  5.79 us (7%)
  between operations  1.31 us (2%)
    all_to_all x1, blocking collectives, per_device(): back = lax.all_to_all(back, ('row', 'x'), 0, 0, tiled=True)  25.1 us
    all_to_all x1, blocking collectives, per_device(): blocks = lax.all_to_all(copies, 'z', 0, 0, tiled=True)  18.9 us
    all_to_all x1, blocking collectives, per_device(): partial = lax.all_to_all(partial, ('row', 'x'), 0, 0, tiled=True)  18.6 us
    unnamed x8, local copies, waits for them, and re-layouts  5.79 us
    pallas_call x1, Pallas kernels, per_device(): pl.pallas_call(product_kernel, grid=(ROWS,), in_specs=[smem, smem, pl.Blo...  5.73 us
    pallas_call x1, Pallas kernels, per_device(): pl.pallas_call(place_kernel, grid=(2,), in_specs=[pl.BlockSpec((SLICES //...  1.8 us

profile of v1, /device:TPU:1, one launch (start us, length us, event | category | flops | bytes accessed | tf_op | source)
XLA Modules:
  0.0 79.1 jit_solution(9618598864067209821)
XLA Ops:
  1.3 0.0 copy-start
  1.3 3.4 %copy-done = bf16[2,2,64,32,512]{4,3,2,1,0:T(8,128)(2,1)S(1)} copy-done((bf16[2,2,64,32,512]{4,3,2,1,0:T(8,128)(2,1)S(1)}, bf16[2,2,64,32,512]{4,3,2,1,0:T(8,128)(2,1)}, u32[]{:S(2)}) %copy-start) | copy-done | bytes 8388632
  4.7 0.0 copy-start.1
  4.7 1.0 %copy-done.1 = bf16[2,2,32,2048]{3,2,1,0:T(8,128)(2,1)S(1)} copy-done((bf16[2,2,32,2048]{3,2,1,0:T(8,128)(2,1)S(1)}, bf16[2,2,32,2048]{3,2,1,0:T(8,128)(2,1)}, u32[]{:S(2)}) %copy-start.1) | copy-done | bytes 524312
  5.7 0.0 copy-start.2
  5.7 0.7 copy-done.2
  6.4 0.0 copy-start.3
  6.4 0.7 copy-done.3
  7.1 5.7 %products.1 = bf16[32,48,128]{2,1,0:T(8,128)(2,1)S(1)} custom-call(s32[64]{0:T(128)S(1)} %copy-done.3, s32[1]{0:T(128)S(6)} %copy.7.step_ref, bf16[2,2,64,32,512]{4,3,2,1,0:T(8,128)(2,1)S(1)} %copy-done, bf16[2,2,32,2048]{3,2,1,0:T(8,128)(2,1)S(1)} %copy-done.1, bf16[2,32,32]{2,1,0:T(8,128)(2,1)S(1)} %copy-done.2), custom_call_target="tpu_custom_call" | custom-call | tf_op jit(solution)/shard_map/products/pallas_call | solution.py:193
  12.8 18.6 %all_to_all.15.in_ref = bf16[32,48,128]{2,1,0:T(8,128)(2,1)S(1)} all-to-all(bf16[32,48,128]{2,1,0:T(8,128)(2,1)S(1)} %products.1), channel_id=1, replica_groups=mesh['row'=8,'x'=4,'z'=8] {'row','x'}, dimensions={0} | all-to-all | bytes 786432 | tf_op jit(solution)/shard_map/all_to_all | solution.py:209
  31.4 0.5 finish.1
  31.9 18.9 %all_to_all.16.blocks_ref = bf16[8,128,128]{2,1,0:T(8,128)(2,1)S(1)} all-to-all(bf16[8,128,128]{2,1,0:T(8,128)(2,1)S(1)} %get-tuple-element.4), channel_id=1, replica_groups=mesh['row'=8,'x'=4,'z'=8] {'z'}, dimensions={0} | all-to-all | bytes 524288 | tf_op jit(solution)/shard_map/all_to_all | solution.py:221
  50.8 1.3 %select.1 = bf16[32,160,128]{2,1,0:T(8,128)(2,1)S(1)} custom-call(s32[64]{0:T(128)S(1)} %copy-done.3, bf16[8,128,128]{2,1,0:T(8,128)(2,1)S(1)} %all_to_all.16.blocks_ref, bf16[128,128]{1,0:T(8,128)(2,1)S(1)} %get-tuple-element.5.rows_ref), custom_call_target="tpu_custom_call" | custom-call | tf_op jit(solution)/shard_map/select/pallas_call | solution.py:222
  52.2 25.1 %all_to_all.17.in_ref = bf16[32,160,128]{2,1,0:T(8,128)(2,1)S(1)} all-to-all(bf16[32,160,128]{2,1,0:T(8,128)(2,1)S(1)} %select.1), channel_id=1, replica_groups=mesh['row'=8,'x'=4,'z'=8] {'row','x'}, dimensions={0} | all-to-all | bytes 2621440 | tf_op jit(solution)/shard_map/all_to_all | solution.py:230
  77.3 1.8 %place.1 = (f32[2,2,2,32,512]{4,3,2,1,0:T(8,128)}, bf16[2,2,2,64,1024]{4,3,2,1,0:T(8,128)(2,1)}) custom-call(bf16[32,160,128]{2,1,0:T(8,128)(2,1)S(1)} %all_to_all.17.in_ref), custom_call_target="tpu_custom_call" | custom-call | tf_op jit(solution)/shard_map/place/pallas_call | solution.py:231
Async XLA Ops:
  1.3 3.4 %copy-start = (bf16[2,2,64,32,512]{4,3,2,1,0:T(8,128)(2,1)S(1)}, bf16[2,2,64,32,512]{4,3,2,1,0:T(8,128)(2,1)}, u32[]{:S(2)}) copy-start(bf16[2,2,64,32,512]{4,3,2,1,0:T(8,128)(2,1)} %hist_ref.1) | copy-start | bytes 25165828
  4.7 1.0 %copy-start.1 = (bf16[2,2,32,2048]{3,2,1,0:T(8,128)(2,1)S(1)}, bf16[2,2,32,2048]{3,2,1,0:T(8,128)(2,1)}, u32[]{:S(2)}) copy-start(bf16[2,2,32,2048]{3,2,1,0:T(8,128)(2,1)} %sigma_ref.1) | copy-start | bytes 1572868
  5.7 0.7 copy-start.2
  6.4 0.7 copy-start.3

commit v2 on v1

v2 whole, which is shorter than its diff:
```python
import jax
import jax.numpy as jnp
from jax import lax
from jax.experimental import pallas as pl
from jax.experimental.pallas import tpu as pltpu
from jax.sharding import Mesh, PartitionSpec as P

TB = 8
ORB = 32
ROWS = 8
XS = 4
YS = 4
PARTS = 16
ZS = 8
BF = jnp.bfloat16
F32 = jnp.float32
SLICES = ROWS * XS
DATA = 32
DIAG = 16
SPAN = 512
BACK = 160


def dot(a, b):
    return jnp.dot(a, b, preferred_element_type=F32)


def dot_nt(a, b):
    return lax.dot_general(a, b, (((1,), (1,)), ((), ())), preferred_element_type=F32)


def iota(shape, axis):
    return lax.broadcasted_iota(jnp.int32, shape, axis)


def one_hot(cond):
    return jnp.where(cond, 1.0, 0.0).astype(BF)


def product_kernel(
    step_ref, map_hbm, hist_hbm, sigma_hbm, prop_hbm, other_ref, own_ref,
    map_ref, hist_ref, sigma_ref, prop_ref, left_ref, acc_ref, hist_sem, sem,
):
    chunks = [
        pltpu.make_async_copy(
            hist_hbm.at[:, :, pl.ds(k * TB, TB)], hist_ref.at[k], hist_sem.at[k]
        )
        for k in range(ROWS)
    ]
    small = [
        pltpu.make_async_copy(source, target, sem.at[i])
        for i, (source, target) in enumerate(
            ((map_hbm, map_ref), (sigma_hbm, sigma_ref), (prop_hbm, prop_ref))
        )
    ]
    for copy in small:
        copy.start()
    for copy in chunks[:6]:
        copy.start()
    core = lax.axis_index("core")
    row = lax.axis_index("y") * 2 + core
    own_ref[SPAN:, :] = jnp.zeros((DIAG, 128), F32)
    other_ref[SPAN:, :] = jnp.zeros((DIAG, 128), BF)
    for copy in small:
        copy.wait()
    current = step_ref[0]
    offset = iota((1, TB * ORB), 1) // ORB
    blocks = [map_ref[row * ROWS + k] for k in range(ROWS)]
    for k in range(ROWS):
        times = blocks[k] * TB + offset
        beyond = times > current
        weight_two = jnp.where(beyond, 0.0, jnp.where(times == 0, 0.5, 1.0))
        weight_one = jnp.where(
            beyond, 0.0, jnp.where((times == 0) | (times == current), 0.5, 1.0)
        )
        lanes = slice(k * TB * ORB, (k + 1) * TB * ORB)
        for s, weight in enumerate((weight_one, weight_two)):
            real = (sigma_ref[s, 0, :, lanes].astype(F32) * weight).astype(BF)
            imag = (sigma_ref[s, 1, :, lanes].astype(F32) * weight).astype(BF)
            upper = slice(s * 2 * ORB, s * 2 * ORB + ORB)
            lower = slice(s * 2 * ORB + ORB, (s + 1) * 2 * ORB)
            left_ref[k, upper, : TB * ORB] = imag
            left_ref[k, lower, : TB * ORB] = -real
            left_ref[k, upper, TB * ORB :] = real
            left_ref[k, lower, TB * ORB :] = imag

    def holder(time):
        at = sum(jnp.where(blocks[k] == time // TB, k + 1, 0) for k in range(ROWS))
        return at > 0, jnp.maximum(at - 1, 0)

    holds_next, chunk_next = holder(current + 1)
    holds_now, chunk_now = holder(current)

    @pl.when(holds_next)
    def _():
        first = (current + 1) % TB * ORB
        lanes = pl.ds(pl.multiple_of(chunk_next * TB * ORB, TB * ORB), TB * ORB)
        pick = one_hot(iota((TB * ORB, 128), 0) == first + iota((TB * ORB, 128), 1) % ORB)
        tiled = dot(sigma_ref[1, :, :, lanes].reshape(2 * ORB, TB * ORB), pick)
        own = iota((2 * ORB, 128), 1) // ORB == iota((2 * ORB, 128), 0) % 4
        fold = one_hot(iota((DIAG, 2 * ORB), 1) // 4 == iota((DIAG, 2 * ORB), 0))
        diag = dot(fold, jnp.where(own, tiled, 0.0).astype(BF)) * 0.5
        own_ref[SPAN:, :] = diag
        other_ref[SPAN:, :] = diag.astype(BF)

    for k in range(ROWS):
        chunks[k].wait()
        if k + 6 < ROWS:
            chunks[k + 6].start()
        for kind in range(2):
            part = dot(left_ref[k], hist_ref[k, kind].reshape(2 * TB * ORB, hist_ref.shape[-1]))
            if k == 0:
                acc_ref[kind] = part
            else:
                acc_ref[kind] += part

    @pl.when(holds_now)
    def _():
        at = current % TB
        real, imag = prop_ref[0], prop_ref[1]
        by_real = jnp.concatenate([real, imag], axis=0)
        by_imag = jnp.concatenate([-imag, real], axis=0)
        for kind in range(2):
            acc_ref[kind, : 2 * ORB] += dot(by_real, hist_ref[chunk_now, kind, 0, at]) + dot(
                by_imag, hist_ref[chunk_now, kind, 1, at]
            )

    other_ref[:SPAN, :] = acc_ref[1 - core].T.astype(BF)
    own_ref[:SPAN, :] = acc_ref[core].T


def join_kernel(own_ref, other_ref, out_ref):
    total = (own_ref[...] + other_ref[...].astype(F32)).astype(BF)
    for part in range(PARTS):
        for blk in range(2):
            first = (blk * PARTS + part) * 16
            out_ref[part, blk * 16 : blk * 16 + 16, :] = total[first : first + 16]
        out_ref[part, DATA:, :] = total[SPAN:]


def finish_kernel(in_ref, prop_ref, rows_ref, mirror_ref):
    sums = []
    for x in range(XS):
        total = in_ref[x, :DATA].astype(F32)
        for r in range(1, YS):
            total += in_ref[r * XS + x, :DATA].astype(F32)
        sums.append(total)
    total = jnp.concatenate(sums, axis=0)
    packed = in_ref[0, DATA:].astype(F32)
    for r in range(1, YS):
        packed += in_ref[r * XS, DATA:].astype(F32)
    lane = iota((ORB, 128), 1)
    left, right = lane < ORB, (lane >= ORB) & (lane < 2 * ORB)
    nothing = jnp.zeros((2 * ORB, 128), F32)

    def matrix(upper_left, upper_right, lower_left, lower_right):
        upper = jnp.where(left, upper_left, jnp.where(right, upper_right, 0.0))
        lower = jnp.where(left, lower_left, jnp.where(right, lower_right, 0.0))
        return jnp.concatenate([nothing, upper, lower], axis=0).astype(BF)

    tile = one_hot(iota((ORB, 128), 0) == iota((ORB, 128), 1) % ORB)
    real, imag = dot(prop_ref[0], tile), dot(prop_ref[1], tile)
    propagate = matrix(real, -imag, imag, real)
    spread = one_hot(iota((2 * ORB, DIAG), 0) // 4 == iota((2 * ORB, DIAG), 1))
    own = iota((2 * ORB, 128), 1) // ORB == iota((2 * ORB, 128), 0) % 4
    wide = jnp.where(own, dot(spread, packed.astype(BF)), 0.0).astype(BF)
    wrap = one_hot(iota((128, 128), 0) % ORB == iota((128, 128), 1) % ORB)
    diag = dot(wide, wrap)
    d_real, d_imag = diag[:ORB], diag[ORB:]
    turn = matrix(d_imag, d_real, -d_real, d_imag)
    low = total.astype(BF)
    new = (total + dot_nt(low, propagate) + dot_nt(low, turn)).astype(BF)
    rows_ref[...] = new
    size = XS * DATA
    lane_block = iota((size, 128), 1) // ORB
    place = iota((size, 128), 0) % 4
    signed = jnp.where(lane_block % 2 == 0, -new.astype(F32), new.astype(F32))
    result = jnp.where(lane_block == place, signed, 0.0)
    for d in range(1, 4):
        moved = jnp.where(lane_block == place, pltpu.roll(signed, 128 - ORB * d, 1), 0.0)
        result += jnp.where(
            place >= d, pltpu.roll(moved, d, 0), pltpu.roll(moved, size + d - 4, 0)
        )
    result = result.astype(BF)
    for z in range(ZS):
        mirror_ref[z] = result


def select_kernel(map_ref, blocks_ref, rows_ref, out_ref):
    for r in range(ROWS):
        for j in range(TB):
            block = map_ref[r * TB + j]
            column = block // 2
            start = pl.multiple_of(column // ZS * DATA + block % 2 * 16, 16)
            piece = blocks_ref[column % ZS, pl.ds(start, 16), :]
            for x in range(XS):
                out_ref[r * XS + x, j * 16 : j * 16 + 16, :] = piece
        for x in range(XS):
            out_ref[r * XS + x, 128:, :] = rows_ref[x * DATA : x * DATA + DATA, :]


def place_kernel(in_ref, rows_ref, mirror_ref, mixed_ref, tall_ref):
    for h in range(2):
        for pair in range(4):
            for half in range(2):
                j = pair * 2 + half
                for tm in range(TB):
                    mixed_ref[h, pair, pl.ds(half * 8 + tm, 16, stride=16), :] = in_ref[
                        tm // 2, 0, tm % 2 * 2 + h, j * 16 : j * 16 + 16, :
                    ].astype(F32)
            for q in range(4):
                for g in range(4):
                    first = (q * 4 + g) * 16
                    mirror_ref[
                        g // 2, 0, g % 2, pair * 16 : pair * 16 + 16, (h * 4 + q) * 128 : (h * 4 + q) * 128 + 128
                    ] = mixed_ref[h, pair, first : first + 16, :].astype(BF)
    for blk in range(2):
        for part in range(16):
            first = (blk * 16 + part) * 16
            tall_ref[first : first + 16, :] = in_ref[
                part // XS, 0, part % XS, 128 + blk * 16 : 144 + blk * 16, :
            ].astype(F32)
    wide = tall_ref[...].T
    for g in range(4):
        rows_ref[g // 2, 0, g % 2] = wide[g * ORB : g * ORB + ORB, :]


def per_device(history, sigma_rows, propagator, block_map, step_index):
    smem = pl.BlockSpec(memory_space=pltpu.SMEM)
    vmem = pl.BlockSpec(memory_space=pltpu.VMEM)
    columns = history.shape[4]
    hbm = pl.BlockSpec(memory_space=pltpu.HBM)
    small = pltpu.CompilerParams(vmem_limit_bytes=16 << 20)
    inputs = (block_map, history, sigma_rows, propagator)
    other, own = pl.pallas_call(
        product_kernel,
        in_specs=[smem] + [hbm] * 4,
        out_specs=[vmem, vmem],
        out_shape=[
            jax.ShapeDtypeStruct((SPAN + DIAG, 128), BF),
            jax.ShapeDtypeStruct((SPAN + DIAG, 128), F32),
        ],
        scratch_shapes=[
            pltpu.SMEM(block_map.shape, jnp.int32),
            pltpu.VMEM((ROWS, 2, 2, TB, ORB, columns), BF),
            pltpu.VMEM(sigma_rows.shape, BF),
            pltpu.VMEM(propagator.shape, BF),
            pltpu.VMEM((ROWS, 128, 2 * TB * ORB), BF),
            pltpu.VMEM((2, 128, columns), F32),
            pltpu.SemaphoreType.DMA((ROWS,)),
            pltpu.SemaphoreType.DMA((3,)),
        ],
        compiler_params=pltpu.CompilerParams(vmem_limit_bytes=40 << 20),
        name="products",
    )(step_index, *(pltpu.with_memory_space_constraint(a, pltpu.HBM) for a in inputs))
    other = lax.ppermute(other, "core", ((0, 1), (1, 0)))
    partial = pl.pallas_call(
        join_kernel,
        in_specs=[vmem] * 2,
        out_specs=vmem,
        out_shape=jax.ShapeDtypeStruct((PARTS, DATA + DIAG, 128), BF),
        compiler_params=small,
        name="join",
    )(own, other)
    partial = lax.all_to_all(partial, ("y", "x"), 0, 0, tiled=True)
    new, copies = pl.pallas_call(
        finish_kernel,
        in_specs=[vmem, vmem],
        out_specs=[vmem, vmem],
        out_shape=[
            jax.ShapeDtypeStruct((XS * DATA, 128), BF),
            jax.ShapeDtypeStruct((ZS, XS * DATA, 128), BF),
        ],
        compiler_params=pltpu.CompilerParams(vmem_limit_bytes=16 << 20),
        name="finish",
    )(partial, propagator)
    blocks = lax.all_to_all(copies, "z", 0, 0, tiled=True)
    back = pl.pallas_call(
        select_kernel,
        in_specs=[smem, vmem, vmem],
        out_specs=vmem,
        out_shape=jax.ShapeDtypeStruct((SLICES, BACK, 128), BF),
        compiler_params=pltpu.CompilerParams(vmem_limit_bytes=16 << 20),
        name="select",
    )(block_map, blocks, new)
    back = lax.all_to_all(back, ("y", "core", "x"), 0, 0, tiled=True)
    back = back.reshape(YS, 2, XS, BACK, 128)
    new_rows, mirror = pl.pallas_call(
        place_kernel,
        grid=(2,),
        in_specs=[pl.BlockSpec((YS, 1, XS, BACK, 128), lambda kind: (0, kind, 0, 0, 0))],
        out_specs=[
            pl.BlockSpec((2, 1, 2, ORB, columns), lambda kind: (0, kind, 0, 0, 0)),
            pl.BlockSpec((2, 1, 2, ROWS * TB, ORB * ORB), lambda kind: (0, kind, 0, 0, 0)),
        ],
        out_shape=[
            jax.ShapeDtypeStruct((2, 2, 2, ORB, columns), F32),
            jax.ShapeDtypeStruct((2, 2, 2, ROWS * TB, ORB * ORB), BF),
        ],
        scratch_shapes=[pltpu.VMEM((2, 4, 256, 128), F32), pltpu.VMEM((columns, 128), F32)],
        compiler_params=pltpu.CompilerParams(vmem_limit_bytes=16 << 20),
        name="place",
    )(back)
    return new_rows, mirror


def solution(mesh):
    split = Mesh(mesh.devices.reshape(YS, 2, XS, ZS), ("y", "core", "x", "z"))
    row = ("y", "core")
    column = ("x", "z")
    return jax.shard_map(
        per_device,
        mesh=split,
        in_specs=(P(None, None, row, None, column), P(None, None, None, row), P(), P(), P()),
        out_specs=(P(None, None, None, None, column), P(None, None, None, row, None)),
        check_vma=False,
    )
```

time: 79.4 us -> 71.4 us (0.90)
  blocking collectives: 62.6 us -> 56.6 us
  local copies, waits for them, and re-layouts: 5.79 us -> 0.01 us
  starting transfers between devices: 0 us -> 3.33 us
  waiting for transfers between devices: 0 us -> 0.99 us
    unnamed x8 -> x4, local copies, waits for them, and re-layouts: 5.79 us -> 0.01 us
    all_to_all x2, blocking collectives: 43.7 us -> 39.4 us  [the longest x1 27.1 us: per_device(): back = lax.all_to_all(back, ('y', 'core', 'x'), 0, 0, tiled=True)]
    ppermute x0 -> x1, starting transfers between devices: none -> 3.33 us  [per_device(): other = lax.ppermute(other, 'core', ((0, 1), (1, 0)))]
    all_to_all x1, blocking collectives: 18.9 us -> 17.2 us  [per_device(): blocks = lax.all_to_all(copies, 'z', 0, 0, tiled=True)]
    ppermute x0 -> x1, waiting for transfers between devices: none -> 0.99 us  [per_device(): other = lax.ppermute(other, 'core', ((0, 1), (1, 0)))]
    pallas_call x2 -> x3, Pallas kernels: 7.53 us -> 7 us  [the longest x1 4.94 us: per_device(): pl.pallas_call(product_kernel, in_specs=[smem] + [hbm] * 4, out_specs=[vm...]
  transfers between devices with their start and end apart: 0 -> 1, of which waited for: 0 -> 1; matrix products, arithmetic and copies ran while one was open for 0% -> 0% of each run, Pallas kernels for 0% -> 0%
where the time goes in v2:
time: 71.4 us; the launch traced here: 71.1 us
  blocking collectives  56.6 us (79%)
  Pallas kernels  8.87 us (12%)
  starting transfers between devices  3.33 us (5%)
  between operations  1.32 us (2%)
  waiting for transfers between devices  0.99 us (1%)
    all_to_all x1, blocking collectives, per_device(): back = lax.all_to_all(back, ('y', 'core', 'x'), 0, 0, tiled=True)  27.1 us
    all_to_all x1, blocking collectives, per_device(): blocks = lax.all_to_all(copies, 'z', 0, 0, tiled=True)  17.2 us
    all_to_all x1, blocking collectives, per_device(): partial = lax.all_to_all(partial, ('y', 'x'), 0, 0, tiled=True)  12.3 us
    pallas_call x1, Pallas kernels, per_device(): pl.pallas_call(product_kernel, in_specs=[smem] + [hbm] * 4, out_specs=[vm...  4.94 us
    ppermute x1, starting transfers between devices, per_device(): other = lax.ppermute(other, 'core', ((0, 1), (1, 0)))  3.33 us
    pallas_call x1, Pallas kernels, per_device(): pl.pallas_call(place_kernel, grid=(2,), in_specs=[pl.BlockSpec((YS, 1, XS...  2.03 us
  transfers between devices with their start and end apart: 1, of which 1 were waited for; matrix products, arithmetic and copies ran while one was open for 0% of the time, Pallas kernels for 0%

profile of v2, /device:TPU:1, one launch (start us, length us, event | category | flops | bytes accessed | tf_op | source)
XLA Modules:
  0.0 71.1 jit_solution(11089064066016269272)
XLA Ops:
  1.3 0.0 copy-start
  1.3 4.9 %products.1 = (bf16[528,128]{1,0:T(8,128)(2,1)S(1)}, f32[528,128]{1,0:T(8,128)S(1)}) custom-call(s32[1]{0:T(128)S(6)} %copy.7.step_ref, s32[64]{0:T(128)} %map_ref.1, bf16[2,2,64,32,512]{4,3,2,1,0:T(8,128)(2,1)} %hist_hbm.1, bf16[2,2,32,2048]{3,2,1,0:T(8,128)(2,1)} %sigma_hbm.1, bf16[2,32,32]{2,1,0:T(8,128)(2,1)} %prop_ref.1), custom_call_target="tpu_custom_call" | custom-call | tf_op jit(solution)/shard_map/products/pallas_call | solution.py:235
  6.2 0.0 copy-start.1
  6.2 3.3 %collective-permute-start = (bf16[528,128]{1,0:T(8,128)(2,1)S(1)}, bf16[528,128]{1,0:T(8,128)(2,1)S(1)}, u32[]{:S(2)}, u32[]{:S(2)}) collective-permute-start(bf16[528,128]{1,0:T(8,128)(2,1)S(1)} %get-tuple-element.7), channel_id=1, source_target_pairs={{0,32},{32,0},{1,33},{33,1},{2,34},{34,2},{3,35},{35,3},{4,36},{36... | collective-permute-start | bytes 405512 | tf_op jit(solution)/shard_map/ppermute | solution.py:256
  9.6 1.0 %collective-permute-done.other_ref = bf16[528,128]{1,0:T(8,128)(2,1)S(1)} collective-permute-done((bf16[528,128]{1,0:T(8,128)(2,1)S(1)}, bf16[528,128]{1,0:T(8,128)(2,1)S(1)}, u32[]{:S(2)}, u32[]{:S(2)}) %collective-permute-start) | collective-permute-done | bytes 135200 | tf_op jit(solution)/shard_map/ppermute | solution.py:256
  10.6 12.3 %all_to_all.15.in_ref = bf16[16,48,128]{2,1,0:T(8,128)(2,1)S(1)} all-to-all(bf16[16,48,128]{2,1,0:T(8,128)(2,1)S(1)} %join.1), channel_id=1, replica_groups=mesh['y'=4,'core'=2,'x'=4,'z'=8] {'y','x'}, dimensions={0} | all-to-all | bytes 393216 | tf_op jit(solution)/shard_map/all_to_all | solution.py:265
  22.9 0.0 copy-done
  22.9 0.5 finish.1
  23.5 17.2 %all_to_all.16.blocks_ref = bf16[8,128,128]{2,1,0:T(8,128)(2,1)S(1)} all-to-all(bf16[8,128,128]{2,1,0:T(8,128)(2,1)S(1)} %get-tuple-element.8), channel_id=1, replica_groups=mesh['y'=4,'core'=2,'x'=4,'z'=8] {'z'}, dimensions={0} | all-to-all | bytes 524288 | tf_op jit(solution)/shard_map/all_to_all | solution.py:277
  40.6 0.0 copy-done.1
  40.6 1.3 %select.1 = bf16[32,160,128]{2,1,0:T(8,128)(2,1)S(1)} custom-call(s32[64]{0:T(128)S(1)} %copy-done.1, bf16[8,128,128]{2,1,0:T(8,128)(2,1)S(1)} %all_to_all.16.blocks_ref, bf16[128,128]{1,0:T(8,128)(2,1)S(1)} %get-tuple-element.9.rows_ref), custom_call_target="tpu_custom_call" | custom-call | tf_op jit(solution)/shard_map/select/pallas_call | solution.py:278
  42.0 27.1 %all_to_all.17 = bf16[32,160,128]{2,1,0:T(8,128)(2,1)S(1)} all-to-all(bf16[32,160,128]{2,1,0:T(8,128)(2,1)S(1)} %select.1), channel_id=1, replica_groups=mesh['y'=4,'core'=2,'x'=4,'z'=8] {'y','core','x'}, dimensions={0} | all-to-all | bytes 2621440 | tf_op jit(solution)/shard_map/all_to_all | solution.py:286
  69.1 2.0 %place.1 = (f32[2,2,2,32,512]{4,3,2,1,0:T(8,128)}, bf16[2,2,2,64,1024]{4,3,2,1,0:T(8,128)(2,1)}) custom-call(bf16[4,2,4,160,128]{4,3,2,1,0:T(8,128)(2,1)S(1)} %bitcast.1), custom_call_target="tpu_custom_call" | custom-call | tf_op jit(solution)/shard_map/place/pallas_call | solution.py:288
  (1 shorter events, 0.0 us)
Async XLA Ops:
  1.3 21.6 %copy-start = (bf16[2,32,32]{2,1,0:T(8,128)(2,1)S(1)}, bf16[2,32,32]{2,1,0:T(8,128)(2,1)}, u32[]{:S(2)}) copy-start(bf16[2,32,32]{2,1,0:T(8,128)(2,1)} %prop_ref.1) | copy-start | bytes 12292
  6.2 34.4 %copy-start.1 = (s32[64]{0:T(128)S(1)}, s32[64]{0:T(128)}, u32[]{:S(2)}) copy-start(s32[64]{0:T(128)} %map_ref.1) | copy-start | bytes 772
  6.2 4.3 %collective-permute-start = (bf16[528,128]{1,0:T(8,128)(2,1)S(1)}, bf16[528,128]{1,0:T(8,128)(2,1)S(1)}, u32[]{:S(2)}, u32[]{:S(2)}) collective-permute-start(bf16[528,128]{1,0:T(8,128)(2,1)S(1)} %get-tuple-element.7), channel_id=1, source_target_pairs={{0,32},{32,0},{1,33},{33,1},{2,34},{34,2},{3,35},{35,3},{4,36},{36... | collective-permute-start | bytes 405512 | tf_op jit(solution)/shard_map/ppermute | solution.py:256

commit v3 on v2

--- a/solution.py
+++ b/solution.py
@@ -38,8 +38,8 @@
 
 
 def product_kernel(
-    step_ref, map_hbm, hist_hbm, sigma_hbm, prop_hbm, other_ref, own_ref,
-    map_ref, hist_ref, sigma_ref, prop_ref, left_ref, acc_ref, hist_sem, sem,
+    step_ref, map_hbm, hist_hbm, sigma_hbm, prop_hbm, other_ref, own_ref, map_ref,
+    hist_ref, sigma_ref, prop_ref, left_ref, acc_ref, hist_sem, sem,
 ):
     chunks = [
         pltpu.make_async_copy(
@@ -199,30 +199,44 @@
             out_ref[r * XS + x, 128:, :] = rows_ref[x * DATA : x * DATA + DATA, :]
 
 
-def place_kernel(in_ref, rows_ref, mirror_ref, mixed_ref, tall_ref):
-    for h in range(2):
+def place_kernel(in_ref, rows_hbm, mirror_hbm, mixed_ref, tall_ref, rows_ref, mirror_ref, rows_sem, mirror_sem):
+    copies = []
+
+    def send(source, target, semaphore):
+        copies.append(pltpu.make_async_copy(source, target, semaphore))
+        copies[-1].start()
+
+    for kind in range(2):
+        for blk in range(2):
+            for part in range(PARTS):
+                first = (blk * PARTS + part) * 16
+                tall_ref[kind, first : first + 16, :] = in_ref[
+                    part // XS, kind, part % XS, 128 + blk * 16 : 144 + blk * 16, :
+                ].astype(F32)
+        wide = tall_ref[kind].T
+        for g in range(4):
+            rows_ref[g // 2, kind, g % 2] = wide[g * ORB : g * ORB + ORB, :]
+        send(rows_ref.at[:, kind], rows_hbm.at[:, kind], rows_sem.at[kind])
+    for kind in range(2):
         for pair in range(4):
-            for half in range(2):
-                j = pair * 2 + half
-                for tm in range(TB):
-                    mixed_ref[h, pair, pl.ds(half * 8 + tm, 16, stride=16), :] = in_ref[
-                        tm // 2, 0, tm % 2 * 2 + h, j * 16 : j * 16 + 16, :
-                    ].astype(F32)
-            for q in range(4):
-                for g in range(4):
-                    first = (q * 4 + g) * 16
-                    mirror_ref[
-                        g // 2, 0, g % 2, pair * 16 : pair * 16 + 16, (h * 4 + q) * 128 : (h * 4 + q) * 128 + 128
-                    ] = mixed_ref[h, pair, first : first + 16, :].astype(BF)
-    for blk in range(2):
-        for part in range(16):
-            first = (blk * 16 + part) * 16
-            tall_ref[first : first + 16, :] = in_ref[
-                part // XS, 0, part % XS, 128 + blk * 16 : 144 + blk * 16, :
-            ].astype(F32)
-    wide = tall_ref[...].T
-    for g in range(4):
-        rows_ref[g // 2, 0, g % 2] = wide[g * ORB : g * ORB + ORB, :]
+            for h in range(2):
+                for half in range(2):
+                    j = pair * 2 + half
+                    for tm in range(TB):
+                        mixed_ref[kind, h, pair, pl.ds(half * 8 + tm, 16, stride=16), :] = in_ref[
+                            tm // 2, kind, tm % 2 * 2 + h, j * 16 : j * 16 + 16, :
+                        ].astype(F32)
+                for q in range(4):
+                    for g in range(4):
+                        first = (q * 4 + g) * 16
+                        lanes = slice((h * 4 + q) * 128, (h * 4 + q) * 128 + 128)
+                        mirror_ref[g // 2, kind, g % 2, pair * 16 : pair * 16 + 16, lanes] = mixed_ref[
+                            kind, h, pair, first : first + 16, :
+                        ].astype(BF)
+            own = (slice(None), kind, slice(None), pl.ds(pair * 16, 16))
+            send(mirror_ref.at[own], mirror_hbm.at[own], mirror_sem.at[kind, pair])
+    for copy in copies:
+        copy.wait()
 
 
 def per_device(history, sigma_rows, propagator, block_map, step_index):
@@ -232,16 +246,16 @@
     hbm = pl.BlockSpec(memory_space=pltpu.HBM)
     small = pltpu.CompilerParams(vmem_limit_bytes=16 << 20)
     inputs = (block_map, history, sigma_rows, propagator)
-    other, own = pl.pallas_call(
+    other, own, kept_map = pl.pallas_call(
         product_kernel,
         in_specs=[smem] + [hbm] * 4,
-        out_specs=[vmem, vmem],
+        out_specs=[vmem, vmem, smem],
         out_shape=[
             jax.ShapeDtypeStruct((SPAN + DIAG, 128), BF),
             jax.ShapeDtypeStruct((SPAN + DIAG, 128), F32),
+            pltpu.SMEM(block_map.shape, jnp.int32),
         ],
         scratch_shapes=[
-            pltpu.SMEM(block_map.shape, jnp.int32),
             pltpu.VMEM((ROWS, 2, 2, TB, ORB, columns), BF),
             pltpu.VMEM(sigma_rows.shape, BF),
             pltpu.VMEM(propagator.shape, BF),
@@ -282,23 +296,25 @@
         out_shape=jax.ShapeDtypeStruct((SLICES, BACK, 128), BF),
         compiler_params=pltpu.CompilerParams(vmem_limit_bytes=16 << 20),
         name="select",
-    )(block_map, blocks, new)
+    )(kept_map, blocks, new)
     back = lax.all_to_all(back, ("y", "core", "x"), 0, 0, tiled=True)
     back = back.reshape(YS, 2, XS, BACK, 128)
+    rows_shape = (2, 2, 2, ORB, columns)
+    mirror_shape = (2, 2, 2, ROWS * TB, ORB * ORB)
     new_rows, mirror = pl.pallas_call(
         place_kernel,
-        grid=(2,),
-        in_specs=[pl.BlockSpec((YS, 1, XS, BACK, 128), lambda kind: (0, kind, 0, 0, 0))],
-        out_specs=[
-            pl.BlockSpec((2, 1, 2, ORB, columns), lambda kind: (0, kind, 0, 0, 0)),
-            pl.BlockSpec((2, 1, 2, ROWS * TB, ORB * ORB), lambda kind: (0, kind, 0, 0, 0)),
+        in_specs=[vmem],
+        out_specs=[pl.BlockSpec(memory_space=pl.ANY)] * 2,
+        out_shape=[jax.ShapeDtypeStruct(rows_shape, F32), jax.ShapeDtypeStruct(mirror_shape, BF)],
+        scratch_shapes=[
+            pltpu.VMEM((2, 2, 4, 256, 128), F32),
+            pltpu.VMEM((2, columns, 128), F32),
+            pltpu.VMEM(rows_shape, F32),
+            pltpu.VMEM(mirror_shape, BF),
+            pltpu.SemaphoreType.DMA((2,)),
+            pltpu.SemaphoreType.DMA((2, 4)),
         ],
-        out_shape=[
-            jax.ShapeDtypeStruct((2, 2, 2, ORB, columns), F32),
-            jax.ShapeDtypeStruct((2, 2, 2, ROWS * TB, ORB * ORB), BF),
-        ],
-        scratch_shapes=[pltpu.VMEM((2, 4, 256, 128), F32), pltpu.VMEM((columns, 128), F32)],
-        compiler_params=pltpu.CompilerParams(vmem_limit_bytes=16 << 20),
+        compiler_params=small,
         name="place",
     )(back)
     return new_rows, mirror

time: 71.4 us -> 70.1 us (0.982)
  Pallas kernels: 8.87 us -> 7.99 us
  blocking collectives: 56.6 us -> 55.8 us
    all_to_all x1, blocking collectives: 12.3 us -> 11.5 us  [per_device(): partial = lax.all_to_all(partial, ('y', 'x'), 0, 0, tiled=True)]
where the time goes in v3:
time: 70.1 us; the launch traced here: 69.9 us
  blocking collectives  55.8 us (80%)
  Pallas kernels  7.99 us (11%)
  starting transfers between devices  3.81 us (5%)
  between operations  1.31 us (2%)
  waiting for transfers between devices  0.99 us (1%)
    all_to_all x1, blocking collectives, per_device(): back = lax.all_to_all(back, ('y', 'core', 'x'), 0, 0, tiled=True)  27.1 us
    all_to_all x1, blocking collectives, per_device(): blocks = lax.all_to_all(copies, 'z', 0, 0, tiled=True)  17.2 us
    all_to_all x1, blocking collectives, per_device(): partial = lax.all_to_all(partial, ('y', 'x'), 0, 0, tiled=True)  11.5 us
    pallas_call x1, Pallas kernels, per_device(): pl.pallas_call(product_kernel, in_specs=[smem] + [hbm] * 4, out_specs=[vm...  4.94 us
    ppermute x1, starting transfers between devices, per_device(): other = lax.ppermute(other, 'core', ((0, 1), (1, 0)))  3.81 us
    pallas_call x1, Pallas kernels, per_device(): pl.pallas_call(place_kernel, in_specs=[vmem], out_specs=[pl.BlockSpec(mem...  1.67 us
  transfers between devices with their start and end apart: 1, of which 1 were waited for; matrix products, arithmetic and copies ran while one was open for 0% of the time, Pallas kernels for 0%

profile of v3, /device:TPU:1, one launch (start us, length us, event | category | flops | bytes accessed | tf_op | source)
XLA Modules:
  0.0 69.9 jit_solution(7169941202776770035)
XLA Ops:
  1.3 0.0 copy-start
  1.3 4.9 %products.1 = (bf16[528,128]{1,0:T(8,128)(2,1)S(1)}, f32[528,128]{1,0:T(8,128)S(1)}, s32[64]{0:T(128)S(4)}) custom-call(s32[1]{0:T(128)S(6)} %copy.7.step_ref, s32[64]{0:T(128)} %map_hbm.1, bf16[2,2,64,32,512]{4,3,2,1,0:T(8,128)(2,1)} %hist_hbm.1, bf16[2,2,32,2048]{3,2,1,0:T(8,128)(2,1)} %sigma_hbm.1, bf16[2,32,32]{2,1,0:T(8,128)(2,1)} %prop_ref.1), custom_call_target="tpu_custom_call" | custom-call | tf_op jit(solution)/shard_map/products/pallas_call | solution.py:249
  6.2 3.8 %collective-permute-start = (bf16[528,128]{1,0:T(8,128)(2,1)S(1)}, bf16[528,128]{1,0:T(8,128)(2,1)S(1)}, u32[]{:S(2)}, u32[]{:S(2)}) collective-permute-start(bf16[528,128]{1,0:T(8,128)(2,1)S(1)} %get-tuple-element.9), channel_id=1, source_target_pairs={{0,32},{32,0},{1,33},{33,1},{2,34},{34,2},{3,35},{35,3},{4,36},{36... | collective-permute-start | bytes 405512 | tf_op jit(solution)/shard_map/ppermute | solution.py:270
  10.0 1.0 %collective-permute-done.other_ref = bf16[528,128]{1,0:T(8,128)(2,1)S(1)} collective-permute-done((bf16[528,128]{1,0:T(8,128)(2,1)S(1)}, bf16[528,128]{1,0:T(8,128)(2,1)S(1)}, u32[]{:S(2)}, u32[]{:S(2)}) %collective-permute-start) | collective-permute-done | bytes 135200 | tf_op jit(solution)/shard_map/ppermute | solution.py:270
  11.1 11.5 %all_to_all.15.in_ref = bf16[16,48,128]{2,1,0:T(8,128)(2,1)S(1)} all-to-all(bf16[16,48,128]{2,1,0:T(8,128)(2,1)S(1)} %join.1), channel_id=1, replica_groups=mesh['y'=4,'core'=2,'x'=4,'z'=8] {'y','x'}, dimensions={0} | all-to-all | bytes 393216 | tf_op jit(solution)/shard_map/all_to_all | solution.py:279
  22.6 0.0 copy-done
  22.6 0.5 finish.1
  23.1 17.2 %all_to_all.16.blocks_ref = bf16[8,128,128]{2,1,0:T(8,128)(2,1)S(1)} all-to-all(bf16[8,128,128]{2,1,0:T(8,128)(2,1)S(1)} %get-tuple-element.10), channel_id=1, replica_groups=mesh['y'=4,'core'=2,'x'=4,'z'=8] {'z'}, dimensions={0} | all-to-all | bytes 524288 | tf_op jit(solution)/shard_map/all_to_all | solution.py:291
  40.3 0.8 %select.1 = bf16[32,160,128]{2,1,0:T(8,128)(2,1)S(1)} custom-call(s32[64]{0:T(128)S(4)} %get-tuple-element.7.map_ref, bf16[8,128,128]{2,1,0:T(8,128)(2,1)S(1)} %all_to_all.16.blocks_ref, bf16[128,128]{1,0:T(8,128)(2,1)S(1)} %get-tuple-element.11.rows_ref), custom_call_target="tpu_custom_call" | custom-call | tf_op jit(solution)/shard_map/select/pallas_call | solution.py:292
  41.1 27.1 %all_to_all.17 = bf16[32,160,128]{2,1,0:T(8,128)(2,1)S(1)} all-to-all(bf16[32,160,128]{2,1,0:T(8,128)(2,1)S(1)} %select.1), channel_id=1, replica_groups=mesh['y'=4,'core'=2,'x'=4,'z'=8] {'y','core','x'}, dimensions={0} | all-to-all | bytes 2621440 | tf_op jit(solution)/shard_map/all_to_all | solution.py:300
  68.2 1.7 %place.1 = (f32[2,2,2,32,512]{4,3,2,1,0:T(8,128)}, bf16[2,2,2,64,1024]{4,3,2,1,0:T(8,128)(2,1)}) custom-call(bf16[4,2,4,160,128]{4,3,2,1,0:T(8,128)(2,1)S(1)} %bitcast.1), custom_call_target="tpu_custom_call" | custom-call | tf_op jit(solution)/shard_map/place/pallas_call | solution.py:304
  (1 shorter events, 0.0 us)
Async XLA Ops:
  1.3 21.3 %copy-start = (bf16[2,32,32]{2,1,0:T(8,128)(2,1)S(1)}, bf16[2,32,32]{2,1,0:T(8,128)(2,1)}, u32[]{:S(2)}) copy-start(bf16[2,32,32]{2,1,0:T(8,128)(2,1)} %prop_ref.1) | copy-start | bytes 12292
  6.2 4.8 %collective-permute-start = (bf16[528,128]{1,0:T(8,128)(2,1)S(1)}, bf16[528,128]{1,0:T(8,128)(2,1)S(1)}, u32[]{:S(2)}, u32[]{:S(2)}) collective-permute-start(bf16[528,128]{1,0:T(8,128)(2,1)S(1)} %get-tuple-element.9), channel_id=1, source_target_pairs={{0,32},{32,0},{1,33},{33,1},{2,34},{34,2},{3,35},{35,3},{4,36},{36... | collective-permute-start | bytes 405512 | tf_op jit(solution)/shard_map/ppermute | solution.py:270

commit v4 on v3

--- a/solution.py
+++ b/solution.py
@@ -307,7 +307,7 @@
         out_specs=[pl.BlockSpec(memory_space=pl.ANY)] * 2,
         out_shape=[jax.ShapeDtypeStruct(rows_shape, F32), jax.ShapeDtypeStruct(mirror_shape, BF)],
         scratch_shapes=[
-            pltpu.VMEM((2, 2, 4, 256, 128), F32),
+            pltpu.VMEM((2, 2, 4, 272, 128), F32),
             pltpu.VMEM((2, columns, 128), F32),
             pltpu.VMEM(rows_shape, F32),
             pltpu.VMEM(mirror_shape, BF),

time: 70.1 us -> 70.1 us (level)
  no operation moved by 1% of the time
where the time goes in v4:
time: 70.1 us; the launch traced here: 69.9 us
  blocking collectives  56.3 us (80%)
  Pallas kernels  7.98 us (11%)
  starting transfers between devices  3.33 us (5%)
  between operations  1.31 us (2%)
  waiting for transfers between devices  0.99 us (1%)
    all_to_all x1, blocking collectives, per_device(): back = lax.all_to_all(back, ('y', 'core', 'x'), 0, 0, tiled=True)  27.1 us
    all_to_all x1, blocking collectives, per_device(): blocks = lax.all_to_all(copies, 'z', 0, 0, tiled=True)  17.2 us
    all_to_all x1, blocking collectives, per_device(): partial = lax.all_to_all(partial, ('y', 'x'), 0, 0, tiled=True)  12 us
    pallas_call x1, Pallas kernels, per_device(): pl.pallas_call(product_kernel, in_specs=[smem] + [hbm] * 4, out_specs=[vm...  4.94 us
    ppermute x1, starting transfers between devices, per_device(): other = lax.ppermute(other, 'core', ((0, 1), (1, 0)))  3.33 us
    pallas_call x1, Pallas kernels, per_device(): pl.pallas_call(place_kernel, in_specs=[vmem], out_specs=[pl.BlockSpec(mem...  1.66 us
  transfers between devices with their start and end apart: 1, of which 1 were waited for; matrix products, arithmetic and copies ran while one was open for 0% of the time, Pallas kernels for 0%

profile of v4, /device:TPU:1, one launch (start us, length us, event | category | flops | bytes accessed | tf_op | source)
XLA Modules:
  0.0 69.9 jit_solution(16387902552471028667)
XLA Ops:
  1.3 0.0 copy-start
  1.3 4.9 %products.1 = (bf16[528,128]{1,0:T(8,128)(2,1)S(1)}, f32[528,128]{1,0:T(8,128)S(1)}, s32[64]{0:T(128)S(4)}) custom-call(s32[1]{0:T(128)S(6)} %copy.7.step_ref, s32[64]{0:T(128)} %map_hbm.1, bf16[2,2,64,32,512]{4,3,2,1,0:T(8,128)(2,1)} %hist_hbm.1, bf16[2,2,32,2048]{3,2,1,0:T(8,128)(2,1)} %sigma_hbm.1, bf16[2,32,32]{2,1,0:T(8,128)(2,1)} %prop_ref.1), custom_call_target="tpu_custom_call" | custom-call | tf_op jit(solution)/shard_map/products/pallas_call | solution.py:249
  6.2 3.3 %collective-permute-start = (bf16[528,128]{1,0:T(8,128)(2,1)S(1)}, bf16[528,128]{1,0:T(8,128)(2,1)S(1)}, u32[]{:S(2)}, u32[]{:S(2)}) collective-permute-start(bf16[528,128]{1,0:T(8,128)(2,1)S(1)} %get-tuple-element.9), channel_id=1, source_target_pairs={{0,32},{32,0},{1,33},{33,1},{2,34},{34,2},{3,35},{35,3},{4,36},{36... | collective-permute-start | bytes 405512 | tf_op jit(solution)/shard_map/ppermute | solution.py:270
  9.6 1.0 %collective-permute-done.other_ref = bf16[528,128]{1,0:T(8,128)(2,1)S(1)} collective-permute-done((bf16[528,128]{1,0:T(8,128)(2,1)S(1)}, bf16[528,128]{1,0:T(8,128)(2,1)S(1)}, u32[]{:S(2)}, u32[]{:S(2)}) %collective-permute-start) | collective-permute-done | bytes 135200 | tf_op jit(solution)/shard_map/ppermute | solution.py:270
  10.6 12.0 %all_to_all.15.in_ref = bf16[16,48,128]{2,1,0:T(8,128)(2,1)S(1)} all-to-all(bf16[16,48,128]{2,1,0:T(8,128)(2,1)S(1)} %join.1), channel_id=1, replica_groups=mesh['y'=4,'core'=2,'x'=4,'z'=8] {'y','x'}, dimensions={0} | all-to-all | bytes 393216 | tf_op jit(solution)/shard_map/all_to_all | solution.py:279
  22.6 0.0 copy-done
  22.6 0.5 finish.1
  23.1 17.2 %all_to_all.16.blocks_ref = bf16[8,128,128]{2,1,0:T(8,128)(2,1)S(1)} all-to-all(bf16[8,128,128]{2,1,0:T(8,128)(2,1)S(1)} %get-tuple-element.10), channel_id=1, replica_groups=mesh['y'=4,'core'=2,'x'=4,'z'=8] {'z'}, dimensions={0} | all-to-all | bytes 524288 | tf_op jit(solution)/shard_map/all_to_all | solution.py:291
  40.3 0.8 %select.1 = bf16[32,160,128]{2,1,0:T(8,128)(2,1)S(1)} custom-call(s32[64]{0:T(128)S(4)} %get-tuple-element.7.map_ref, bf16[8,128,128]{2,1,0:T(8,128)(2,1)S(1)} %all_to_all.16.blocks_ref, bf16[128,128]{1,0:T(8,128)(2,1)S(1)} %get-tuple-element.11.rows_ref), custom_call_target="tpu_custom_call" | custom-call | tf_op jit(solution)/shard_map/select/pallas_call | solution.py:292
  41.1 27.1 %all_to_all.17 = bf16[32,160,128]{2,1,0:T(8,128)(2,1)S(1)} all-to-all(bf16[32,160,128]{2,1,0:T(8,128)(2,1)S(1)} %select.1), channel_id=1, replica_groups=mesh['y'=4,'core'=2,'x'=4,'z'=8] {'y','core','x'}, dimensions={0} | all-to-all | bytes 2621440 | tf_op jit(solution)/shard_map/all_to_all | solution.py:300
  68.2 1.7 %place.1 = (f32[2,2,2,32,512]{4,3,2,1,0:T(8,128)}, bf16[2,2,2,64,1024]{4,3,2,1,0:T(8,128)(2,1)}) custom-call(bf16[4,2,4,160,128]{4,3,2,1,0:T(8,128)(2,1)S(1)} %bitcast.1), custom_call_target="tpu_custom_call" | custom-call | tf_op jit(solution)/shard_map/place/pallas_call | solution.py:304
  (1 shorter events, 0.0 us)
Async XLA Ops:
  1.3 21.3 %copy-start = (bf16[2,32,32]{2,1,0:T(8,128)(2,1)S(1)}, bf16[2,32,32]{2,1,0:T(8,128)(2,1)}, u32[]{:S(2)}) copy-start(bf16[2,32,32]{2,1,0:T(8,128)(2,1)} %prop_ref.1) | copy-start | bytes 12292
  6.2 4.3 %collective-permute-start = (bf16[528,128]{1,0:T(8,128)(2,1)S(1)}, bf16[528,128]{1,0:T(8,128)(2,1)S(1)}, u32[]{:S(2)}, u32[]{:S(2)}) collective-permute-start(bf16[528,128]{1,0:T(8,128)(2,1)S(1)} %get-tuple-element.9), channel_id=1, source_target_pairs={{0,32},{32,0},{1,33},{33,1},{2,34},{34,2},{3,35},{35,3},{4,36},{36... | collective-permute-start | bytes 405512 | tf_op jit(solution)/shard_map/ppermute | solution.py:270

commit v5 on v4

--- a/solution.py
+++ b/solution.py
@@ -207,17 +207,6 @@
         copies[-1].start()
 
     for kind in range(2):
-        for blk in range(2):
-            for part in range(PARTS):
-                first = (blk * PARTS + part) * 16
-                tall_ref[kind, first : first + 16, :] = in_ref[
-                    part // XS, kind, part % XS, 128 + blk * 16 : 144 + blk * 16, :
-                ].astype(F32)
-        wide = tall_ref[kind].T
-        for g in range(4):
-            rows_ref[g // 2, kind, g % 2] = wide[g * ORB : g * ORB + ORB, :]
-        send(rows_ref.at[:, kind], rows_hbm.at[:, kind], rows_sem.at[kind])
-    for kind in range(2):
         for pair in range(4):
             for h in range(2):
                 for half in range(2):
@@ -235,6 +224,17 @@
                         ].astype(BF)
             own = (slice(None), kind, slice(None), pl.ds(pair * 16, 16))
             send(mirror_ref.at[own], mirror_hbm.at[own], mirror_sem.at[kind, pair])
+    for kind in range(2):
+        for blk in range(2):
+            for part in range(PARTS):
+                first = (blk * PARTS + part) * 16
+                tall_ref[kind, first : first + 16, :] = in_ref[
+                    part // XS, kind, part % XS, 128 + blk * 16 : 144 + blk * 16, :
+                ].astype(F32)
+        wide = tall_ref[kind].T
+        for g in range(4):
+            rows_ref[g // 2, kind, g % 2] = wide[g * ORB : g * ORB + ORB, :]
+        send(rows_ref.at[:, kind], rows_hbm.at[:, kind], rows_sem.at[kind])
     for copy in copies:
         copy.wait()
 

time: 70.1 us -> 70.4 us (level)
  no operation moved by 1% of the time
where the time goes in v5:
time: 70.4 us; the launch traced here: 70.3 us
  blocking collectives  56.6 us (80%)
  Pallas kernels  8.13 us (12%)
  starting transfers between devices  3.33 us (5%)
  between operations  1.31 us (2%)
  waiting for transfers between devices  0.99 us (1%)
    all_to_all x1, blocking collectives, per_device(): back = lax.all_to_all(back, ('y', 'core', 'x'), 0, 0, tiled=True)  27.1 us
    all_to_all x1, blocking collectives, per_device(): blocks = lax.all_to_all(copies, 'z', 0, 0, tiled=True)  17.2 us
    all_to_all x1, blocking collectives, per_device(): partial = lax.all_to_all(partial, ('y', 'x'), 0, 0, tiled=True)  12.3 us
    pallas_call x1, Pallas kernels, per_device(): pl.pallas_call(product_kernel, in_specs=[smem] + [hbm] * 4, out_specs=[vm...  4.94 us
    ppermute x1, starting transfers between devices, per_device(): other = lax.ppermute(other, 'core', ((0, 1), (1, 0)))  3.33 us
    pallas_call x1, Pallas kernels, per_device(): pl.pallas_call(place_kernel, in_specs=[vmem], out_specs=[pl.BlockSpec(mem...  1.82 us
  transfers between devices with their start and end apart: 1, of which 1 were waited for; matrix products, arithmetic and copies ran while one was open for 0% of the time, Pallas kernels for 0%

profile of v5, /device:TPU:1, one launch (start us, length us, event | category | flops | bytes accessed | tf_op | source)
XLA Modules:
  0.0 70.3 jit_solution(4835135808861672493)
XLA Ops:
  1.3 0.0 copy-start
  1.3 4.9 %products.1 = (bf16[528,128]{1,0:T(8,128)(2,1)S(1)}, f32[528,128]{1,0:T(8,128)S(1)}, s32[64]{0:T(128)S(4)}) custom-call(s32[1]{0:T(128)S(6)} %copy.7.step_ref, s32[64]{0:T(128)} %map_hbm.1, bf16[2,2,64,32,512]{4,3,2,1,0:T(8,128)(2,1)} %hist_hbm.1, bf16[2,2,32,2048]{3,2,1,0:T(8,128)(2,1)} %sigma_hbm.1, bf16[2,32,32]{2,1,0:T(8,128)(2,1)} %prop_ref.1), custom_call_target="tpu_custom_call" | custom-call | tf_op jit(solution)/shard_map/products/pallas_call | solution.py:249
  6.2 3.3 %collective-permute-start = (bf16[528,128]{1,0:T(8,128)(2,1)S(1)}, bf16[528,128]{1,0:T(8,128)(2,1)S(1)}, u32[]{:S(2)}, u32[]{:S(2)}) collective-permute-start(bf16[528,128]{1,0:T(8,128)(2,1)S(1)} %get-tuple-element.9), channel_id=1, source_target_pairs={{0,32},{32,0},{1,33},{33,1},{2,34},{34,2},{3,35},{35,3},{4,36},{36... | collective-permute-start | bytes 405512 | tf_op jit(solution)/shard_map/ppermute | solution.py:270
  9.6 1.0 %collective-permute-done.other_ref = bf16[528,128]{1,0:T(8,128)(2,1)S(1)} collective-permute-done((bf16[528,128]{1,0:T(8,128)(2,1)S(1)}, bf16[528,128]{1,0:T(8,128)(2,1)S(1)}, u32[]{:S(2)}, u32[]{:S(2)}) %collective-permute-start) | collective-permute-done | bytes 135200 | tf_op jit(solution)/shard_map/ppermute | solution.py:270
  10.6 12.3 %all_to_all.15.in_ref = bf16[16,48,128]{2,1,0:T(8,128)(2,1)S(1)} all-to-all(bf16[16,48,128]{2,1,0:T(8,128)(2,1)S(1)} %join.1), channel_id=1, replica_groups=mesh['y'=4,'core'=2,'x'=4,'z'=8] {'y','x'}, dimensions={0} | all-to-all | bytes 393216 | tf_op jit(solution)/shard_map/all_to_all | solution.py:279
  22.9 0.0 copy-done
  22.9 0.5 finish.1
  23.4 17.2 %all_to_all.16.blocks_ref = bf16[8,128,128]{2,1,0:T(8,128)(2,1)S(1)} all-to-all(bf16[8,128,128]{2,1,0:T(8,128)(2,1)S(1)} %get-tuple-element.10), channel_id=1, replica_groups=mesh['y'=4,'core'=2,'x'=4,'z'=8] {'z'}, dimensions={0} | all-to-all | bytes 524288 | tf_op jit(solution)/shard_map/all_to_all | solution.py:291
  40.6 0.8 %select.1 = bf16[32,160,128]{2,1,0:T(8,128)(2,1)S(1)} custom-call(s32[64]{0:T(128)S(4)} %get-tuple-element.7.map_ref, bf16[8,128,128]{2,1,0:T(8,128)(2,1)S(1)} %all_to_all.16.blocks_ref, bf16[128,128]{1,0:T(8,128)(2,1)S(1)} %get-tuple-element.11.rows_ref), custom_call_target="tpu_custom_call" | custom-call | tf_op jit(solution)/shard_map/select/pallas_call | solution.py:292
  41.4 27.1 %all_to_all.17 = bf16[32,160,128]{2,1,0:T(8,128)(2,1)S(1)} all-to-all(bf16[32,160,128]{2,1,0:T(8,128)(2,1)S(1)} %select.1), channel_id=1, replica_groups=mesh['y'=4,'core'=2,'x'=4,'z'=8] {'y','core','x'}, dimensions={0} | all-to-all | bytes 2621440 | tf_op jit(solution)/shard_map/all_to_all | solution.py:300
  68.5 1.8 %place.1 = (f32[2,2,2,32,512]{4,3,2,1,0:T(8,128)}, bf16[2,2,2,64,1024]{4,3,2,1,0:T(8,128)(2,1)}) custom-call(bf16[4,2,4,160,128]{4,3,2,1,0:T(8,128)(2,1)S(1)} %bitcast.1), custom_call_target="tpu_custom_call" | custom-call | tf_op jit(solution)/shard_map/place/pallas_call | solution.py:304
  (1 shorter events, 0.0 us)
Async XLA Ops:
  1.3 21.6 %copy-start = (bf16[2,32,32]{2,1,0:T(8,128)(2,1)S(1)}, bf16[2,32,32]{2,1,0:T(8,128)(2,1)}, u32[]{:S(2)}) copy-start(bf16[2,32,32]{2,1,0:T(8,128)(2,1)} %prop_ref.1) | copy-start | bytes 12292
  6.2 4.3 %collective-permute-start = (bf16[528,128]{1,0:T(8,128)(2,1)S(1)}, bf16[528,128]{1,0:T(8,128)(2,1)S(1)}, u32[]{:S(2)}, u32[]{:S(2)}) collective-permute-start(bf16[528,128]{1,0:T(8,128)(2,1)S(1)} %get-tuple-element.9), channel_id=1, source_target_pairs={{0,32},{32,0},{1,33},{33,1},{2,34},{34,2},{3,35},{35,3},{4,36},{36... | collective-permute-start | bytes 405512 | tf_op jit(solution)/shard_map/ppermute | solution.py:270
